TPU v7x, 32 devices: a whole 2x2x4 slice. The times are simulated.
32 devices in a mesh: mode: 4 (over y, core), mesh: 8 (over z, x).
Axes of the slice: x: 2, y: 2, z: 4, core: 2. Of those that a mesh axis runs over, the one named last changes fastest.
Arguments:
- src_rows: bfloat16 [8192, 640], P(('mode', 'mesh')), parts along dimension 0, may hold values from -4 to 4
- src_owner: int32 [8192, 1], P(('mode', 'mesh')), parts along dimension 0, may hold values from 0 to 7; in each aligned block of 256 rows (0 to 255, 256 to 511, ...) at most 64 rows name the same one
- src_slot: int32 [8192], P(('mode', 'mesh')), parts along dimension 0, may hold values from 0 to 63
- neighbour_offset: int32 [2048, 6], P(('mode', 'mesh')), parts along dimension 0, may hold values from -16 to 16
- liner_face: int32 [2048], P(('mode', 'mesh')), parts along dimension 0, may hold values from 0 to 127
- admittance: float32 [8, 128], P('mode', 'mesh'), parts along dimension 0, may hold values from 0.2 to 1.5
- observe_weight: float32 [2048], P(('mode', 'mesh')), parts along dimension 0, may hold values from 0.3 to 3
- coupling: bfloat16 [24, 320, 640], P('mode'), parts along dimension 0, may hold values from -0.046875 to 0.046875
- block_inv: bfloat16 [1280, 640], P('mode'), parts along dimension 0, may hold values from -1.5 to 1.5, as said below
- liner_op: bfloat16 [1280, 640], P('mode'), parts along dimension 0, may hold values from -0.0625 to 0.0625
Outputs:
- state_field: bfloat16 [2048, 640], P(('mode', 'mesh')), parts along dimension 0
- adjoint_field: bfloat16 [2048, 640], P(('mode', 'mesh')), parts along dimension 0
- liner_grad: float32 [8, 128], P('mode', 'mesh'), parts along dimension 0
There are 4 independent parts, one for each index of `mode`. A program takes and returns all parts, laid end to end along the dimension named above; each array names one. Nothing has to cross between parts.
Inputs may be any that keep to these rules, and one draw needn't show every extreme that they name: `src_owner`: in the rows of one device no owner is named by more than 64 rows, a bound that some block reaches. `block_inv`: real parts of the diagonal entries lie near 0.8; the rest is of order 320 ** -0.5.
All inputs are finite; a program needn't handle non-finite values.
Results may differ from a plain program's by a relative error of at most 0.018.
Values may be sent and summed in bfloat16 or wider, within the bound.
A program may use at most 64 MiB of HBM per device.

v0:
```python
import functools

import jax
import jax.numpy as jnp
from jax import lax
from jax.experimental import pallas as pl
from jax.experimental.pallas import tpu as pltpu
from jax.sharding import PartitionSpec as P

SWEEPS = 4
RIM = 16
DEEP = 2 * RIM
FACES = 6
HALF = 384
FULL = 2 * HALF
MESH = pl.DeviceIdType.MESH
F32 = jnp.float32
BF16 = jnp.bfloat16


def iota(shape, dim):
    return lax.broadcasted_iota(jnp.int32, shape, dim)


def dot(a, b):
    return jnp.dot(a, b, preferred_element_type=F32)


def widen(x, nb):
    rows = x.shape[0]
    turned = pltpu.roll(x, HALF - nb, 1)
    wrap = 2 * (HALF - nb)
    real = jnp.where(iota((rows, HALF), 1) < nb, x[:, :HALF], 0.0)
    last = jnp.where(iota((rows, wrap), 1) < HALF - nb, turned[:, :wrap], 0.0)
    return jnp.concatenate([real, turned[:, HALF:], last], axis=1)


def narrow(x, nb):
    turned = pltpu.roll(x, FULL - (HALF - nb), 1)
    return jnp.where(iota((x.shape[0], 2 * nb), 1) < nb, x[:, : 2 * nb], turned[:, : 2 * nb])


def combine(prod):
    rows = prod.shape[0] // 2
    return (
        prod[:rows, :HALF] - prod[rows:, HALF:],
        prod[:rows, HALF:] + prod[rows:, :HALF],
    )


def halves(x):
    return jnp.concatenate([x[:, :HALF], x[:, HALF:]], axis=0)


def column(row):
    count = row.shape[1]
    same = iota((count, count), 0) == iota((count, count), 1)
    return jnp.sum(jnp.where(same, row, 0.0), axis=1, keepdims=True)


def kernel(
    n,
    owner_ref,
    slot_ref,
    off_ref,
    face_ref,
    adm_ref,
    weight_ref,
    src_ref,
    coupling_hbm,
    inv_hbm,
    liner_hbm,
    state_ref,
    adjoint_ref,
    grad_ref,
    send,
    recv,
    adm_send,
    adm_recv,
    off_send,
    off_halo,
    grad_send,
    grad_recv,
    fields,
    w_fwd,
    w_adj,
    inv_pad,
    inv_herm,
    liner_pad,
    matrix,
    pick_fwd,
    pick_adj,
    src_sems,
    adm_sems,
    off_sems,
    grad_sems,
    halo_sems,
    coupling_ref,
    inv_ref,
    liner_ref,
    load_sems,
):
    me = lax.axis_index("mesh")
    elems = off_ref.shape[1]
    nb = inv_ref.shape[0]
    lin = adm_ref.shape[1]
    rows = src_ref.shape[0]

    loads = [
        pltpu.make_async_copy(hbm, here, load_sems.at[i])
        for i, (hbm, here) in enumerate(
            ((inv_hbm, inv_ref), (liner_hbm, liner_ref), (coupling_hbm, coupling_ref))
        )
    ]
    for load in loads:
        load.start()

    def peer(k):
        return lax.rem(me + k, n)

    def to(src, dst, send_sem, recv_sem, p):
        return pltpu.make_async_remote_copy(
            src_ref=src,
            dst_ref=dst,
            send_sem=send_sem,
            recv_sem=recv_sem,
            device_id={"mesh": p},
            device_id_type=MESH,
        )

    def src_copy(p, owner):
        return to(send.at[p], recv.at[owner], src_sems.at[0, p], src_sems.at[1, owner], p)

    def adm_copy(p, owner):
        return to(adm_send, adm_recv.at[owner], adm_sems.at[0, p], adm_sems.at[1, owner], p)

    def grad_copy(p, owner):
        return to(
            grad_send.at[p], grad_recv.at[owner], grad_sems.at[0, p], grad_sems.at[1, owner], p
        )

    def off_copy(side, p):
        return to(off_send, off_halo.at[side], off_sems.at[0, side], off_sems.at[1, side], p)

    def halo_copy(step, side, p):
        own = pl.ds(elems - DEEP if side == 0 else 0, DEEP)
        there = pl.ds(elems if side == 0 else elems + DEEP, DEEP)
        return to(
            fields.at[step, own],
            fields.at[step, there],
            halo_sems.at[0, step // 2, side],
            halo_sems.at[1, step // 2, side],
            p,
        )

    up, down = jnp.minimum(me + 1, n - 1), jnp.maximum(me - 1, 0)
    has_up, has_down = me < n - 1, me > 0

    fields[...] = jnp.zeros_like(fields)
    off_halo[...] = jnp.zeros_like(off_halo)

    barrier = pltpu.get_barrier_semaphore()

    @pl.loop(1, n)
    def _(k):
        pl.semaphore_signal(barrier, inc=1, device_id={"mesh": peer(k)}, device_id_type=MESH)

    adm_send[...] = jnp.zeros_like(adm_send)
    adm_send[0:2, 0:lin] = adm_ref[...]
    off_send[...] = jnp.zeros_like(off_send)
    off_send[0:FACES, 0:elems] = off_ref[...].astype(F32)
    off_send[FACES : FACES + 1, 0:elems] = face_ref[...].astype(F32)
    target = owner_ref[...] * elems + slot_ref[...]

    def partial_sum(p):
        pick = (iota((elems, rows), 0) + p * elems) == target
        return dot(pick.astype(F32).astype(BF16), src_ref[...])

    @pl.loop(1, n)
    def _(k):
        p = peer(k)
        send[p] = partial_sum(p).astype(BF16)

    pl.semaphore_wait(barrier, n - 1)

    @pl.loop(1, n)
    def _(k):
        src_copy(peer(k), me).start()

    @pl.when(has_up)
    def _():
        off_copy(0, up).start()

    @pl.when(has_down)
    def _():
        off_copy(1, down).start()

    @pl.loop(1, n)
    def _(k):
        adm_copy(peer(k), me).start()

    def padded(x):
        wide = widen(x.astype(F32), nb)
        return jnp.concatenate([wide, jnp.zeros((HALF - nb, FULL), F32)], axis=0)

    for load in loads:
        load.wait()
    inv_wide = padded(inv_ref[...])
    inv_pad[...] = inv_wide.astype(BF16)
    inv_herm[:, :HALF] = inv_wide[:, :HALF].T.astype(BF16)
    inv_herm[:, HALF:] = (-inv_wide[:, HALF:].T).astype(BF16)
    liner_pad[...] = padded(liner_ref[...]).astype(BF16)

    def fold(f):
        at = pl.ds(pl.multiple_of(f * HALF, HALF), HALF)
        re, im = combine(dot(halves(matrix[...]), inv_pad[...]))
        w_fwd[at, :HALF] = re.astype(BF16)
        w_fwd[at, HALF:] = im.astype(BF16)
        re, im = combine(dot(halves(inv_pad[...]), matrix[...]))
        w_adj[at, :HALF] = re.T.astype(BF16)
        w_adj[at, HALF:] = (-im.T).astype(BF16)

    @pl.loop(0, FACES)
    def _(f):
        matrix[...] = padded(coupling_ref[f]).astype(BF16)
        fold(f)

    matrix[...] = liner_pad[...]
    fold(FACES)

    @pl.when(has_down)
    def _():
        off_copy(0, down).wait_recv()

    @pl.when(has_up)
    def _():
        off_copy(1, up).wait_recv()

    lane8 = iota((8, 128), 1)
    offs = jnp.where(
        lane8 < elems,
        off_send[...],
        jnp.where(
            lane8 < elems + DEEP,
            pltpu.roll(off_halo[0], DEEP, 1),
            pltpu.roll(off_halo[1], elems + DEEP, 1),
        ),
    )
    lane = iota((128, 128), 1)
    place_row = jnp.where(
        lane < elems, lane, jnp.where(lane < elems + DEEP, lane - elems - DEEP, lane - DEEP)
    ).astype(F32)
    place_col = place_row.T
    near = elems + DEEP - RIM

    def kept(x):
        return jnp.concatenate([x[:elems], x[near : near + DEEP]], axis=0)

    for f in range(FACES):
        lands = jnp.where(place_col == place_row + offs[f : f + 1, :], 1.0, 0.0)
        pick_adj[f] = kept(lands).astype(BF16)
        pick_fwd[f] = kept(lands.T).astype(BF16)

    face_all = kept(column(offs[FACES : FACES + 1, :]))
    face = face_all[:elems]
    weight = column(weight_ref[...])
    lane_e = iota((elems, 128), 1)

    lane_a = iota((elems + DEEP, 128), 1)

    def face_pick(p):
        return jnp.logical_and(face == (lane_e + p * lin).astype(F32), lane_e < lin)

    def admit(table, p, sums):
        pick = jnp.logical_and(face_all == (lane_a + p * lin).astype(F32), lane_a < lin)
        return tuple(s + jnp.where(pick, table[i : i + 1, :], 0.0) for i, s in enumerate(sums))

    def admit_peer(k, sums):
        p = peer(n - k)
        adm_copy(p, p).wait_recv()
        return admit(adm_recv[p], p, sums)

    sums = admit(adm_send[...], me, (jnp.zeros((elems + DEEP, 128), F32),) * 2)
    sums = lax.fori_loop(1, n, admit_peer, sums)
    y_re = jnp.sum(sums[0], axis=1, keepdims=True)
    y_im = jnp.sum(sums[1], axis=1, keepdims=True)

    def take(k, total):
        p = peer(n - k)
        src_copy(p, p).wait_recv()
        return total + recv[p].astype(F32)

    forcing = widen(lax.fori_loop(1, n, take, partial_sum(me)), nb)

    def sweeps(first, start, pick_ref, w_ref, yi, beside):
        def sweep(s, pick, u, y_r, y_i):
            count = u.shape[0]
            u_re, u_im = u[:, :HALF], u[:, HALF:]
            wall = jnp.concatenate([y_r * u_re - y_i * u_im, y_r * u_im + y_i * u_re], axis=0)
            met = dot(pick.reshape(FACES * count, 128), fields[s]).astype(BF16)
            parts = [halves(met[f * count : (f + 1) * count]) for f in range(FACES)]
            left = jnp.concatenate(parts + [wall.astype(BF16)], axis=1)
            return jnp.concatenate(combine(dot(left, w_ref[...])), axis=1)

        start = jnp.concatenate(start, axis=1)
        now = start.astype(BF16)
        start_near = None
        for s in range(first, first + SWEEPS, 2):
            fields[s, 0:elems, :] = now

            @pl.when(has_up)
            def _():
                halo_copy(s, 0, up).start()

            @pl.when(has_down)
            def _():
                halo_copy(s, 1, down).start()

            if s == first:
                beside()

            @pl.when(has_down)
            def _():
                halo_copy(s, 0, down).wait_recv()

            @pl.when(has_up)
            def _():
                halo_copy(s, 1, up).wait_recv()

            halo = fields[s, near : near + DEEP, :].astype(F32)
            if start_near is None:
                start_near = jnp.concatenate([start, halo], axis=0)
            u = jnp.concatenate([now.astype(F32), halo], axis=0)
            now = (start_near - sweep(s, pick_ref[...], u, y_re, yi)).astype(BF16)
            fields[s + 1, 0:elems, :] = now[:elems]
            fields[s + 1, near : near + DEEP, :] = now[elems:]
            u = now[:elems].astype(F32)
            now = start - sweep(s + 1, pick_ref[:, 0:elems, :], u, y_re[:elems], yi[:elems])
            now = now.astype(BF16)
        return now

    start = combine(dot(halves(forcing.astype(BF16)), inv_pad[...]))
    state = sweeps(0, start, pick_fwd, w_fwd, y_im, lambda: None)
    state_f = state.astype(F32)
    source = weight * state_f
    start = combine(dot(halves(source.astype(BF16)), inv_herm[...]))
    walls = []

    def beside():
        state_ref[...] = narrow(state_f, nb).astype(BF16)
        walls.extend(combine(dot(halves(state), liner_pad[...])))

    adjoint = sweeps(SWEEPS, start, pick_adj, w_adj, -y_im, beside)
    adjoint_f = adjoint.astype(F32)
    wall_re, wall_im = walls
    a, b = adjoint_f[:, :HALF], adjoint_f[:, HALF:]
    term_re = -jnp.sum(a * wall_re + b * wall_im, axis=1, keepdims=True) / 16.0
    term_im = -jnp.sum(b * wall_re - a * wall_im, axis=1, keepdims=True) / 16.0

    def grad_part(p):
        pick = face_pick(p)
        re = jnp.sum(jnp.where(pick, term_re, 0.0), axis=0, keepdims=True)
        im = jnp.sum(jnp.where(pick, term_im, 0.0), axis=0, keepdims=True)
        return jnp.concatenate([re, im, jnp.zeros((6, 128), F32)], axis=0)

    @pl.loop(1, n)
    def _(k):
        p = peer(k)
        grad_send[p] = grad_part(p)
        grad_copy(p, me).start()

    def take_grad(k, total):
        p = peer(n - k)
        grad_copy(p, p).wait_recv()
        return total + grad_recv[p]

    adjoint_ref[...] = narrow(adjoint_f, nb).astype(BF16)
    total = lax.fori_loop(1, n, take_grad, grad_part(me))
    grad_ref[...] = total[0:2, 0:lin]

    @pl.loop(1, n)
    def _(k):
        p = peer(k)
        src_copy(p, me).wait_send()
        adm_copy(p, me).wait_send()
        grad_copy(p, me).wait_send()

    @pl.when(has_up)
    def _():
        off_copy(0, up).wait_send()
        for s in range(0, 2 * SWEEPS, 2):
            halo_copy(s, 0, up).wait_send()

    @pl.when(has_down)
    def _():
        off_copy(1, down).wait_send()
        for s in range(0, 2 * SWEEPS, 2):
            halo_copy(s, 1, down).wait_send()


def solution(mesh):
    n = mesh.shape["mesh"]

    def local(
        src_rows,
        src_owner,
        src_slot,
        neighbour_offset,
        liner_face,
        admittance,
        observe_weight,
        coupling,
        block_inv,
        liner_op,
    ):
        rows, width = src_rows.shape
        elems = liner_face.shape[0]
        lin = admittance.shape[1]
        vmem = pl.BlockSpec(memory_space=pltpu.VMEM)
        dma = pltpu.SemaphoreType.DMA
        return tuple(
            pl.pallas_call(
                functools.partial(kernel, n),
                out_shape=(
                    jax.ShapeDtypeStruct((elems, width), BF16),
                    jax.ShapeDtypeStruct((elems, width), BF16),
                    jax.ShapeDtypeStruct((2, lin), F32),
                ),
                in_specs=[vmem] * 7 + [pl.BlockSpec(memory_space=pltpu.HBM)] * 3,
                out_specs=(vmem,) * 3,
                scratch_shapes=[
                    pltpu.VMEM((n, elems, width), BF16),
                    pltpu.VMEM((n, elems, width), BF16),
                    pltpu.VMEM((8, 128), F32),
                    pltpu.VMEM((n, 8, 128), F32),
                    pltpu.VMEM((8, 128), F32),
                    pltpu.VMEM((2, 8, 128), F32),
                    pltpu.VMEM((n, 8, 128), F32),
                    pltpu.VMEM((n, 8, 128), F32),
                    pltpu.VMEM((2 * SWEEPS, 128, FULL), BF16),
                    pltpu.VMEM(((FACES + 1) * HALF, FULL), BF16),
                    pltpu.VMEM(((FACES + 1) * HALF, FULL), BF16),
                    pltpu.VMEM((HALF, FULL), BF16),
                    pltpu.VMEM((HALF, FULL), BF16),
                    pltpu.VMEM((HALF, FULL), BF16),
                    pltpu.VMEM((HALF, FULL), BF16),
                    pltpu.VMEM((FACES, elems + DEEP, 128), BF16),
                    pltpu.VMEM((FACES, elems + DEEP, 128), BF16),
                    dma((2, n)),
                    dma((2, n)),
                    dma((2, 2)),
                    dma((2, n)),
                    dma((2, SWEEPS, 2)),
                    pltpu.VMEM(coupling.shape, BF16),
                    pltpu.VMEM(block_inv.shape, BF16),
                    pltpu.VMEM(liner_op.shape, BF16),
                    dma((3,)),
                ],
                compiler_params=pltpu.CompilerParams(
                    collective_id=0, has_side_effects=True, vmem_limit_bytes=2**26 - 2**16
                ),
            )(
                src_owner.reshape(1, rows),
                src_slot.reshape(1, rows),
                neighbour_offset.T,
                liner_face.reshape(1, elems),
                admittance,
                observe_weight.reshape(1, elems),
                src_rows,
                coupling,
                block_inv,
                liner_op,
            )
        )

    placed = (
        P(("mode", "mesh"), None),
        P(("mode", "mesh"), None),
        P(("mode", "mesh")),
        P(("mode", "mesh"), None),
        P(("mode", "mesh")),
        P("mode", "mesh"),
        P(("mode", "mesh")),
        P("mode", None, None),
        P("mode", None),
        P("mode", None),
    )
    return jax.shard_map(
        local,
        mesh=mesh,
        in_specs=placed,
        out_specs=(P(("mode", "mesh"), None), P(("mode", "mesh"), None), P("mode", "mesh")),
        check_vma=False,
    )
```

profile of v0, /device:TPU:0, one launch (start us, length us, event | category | flops | bytes accessed | tf_op | source)
XLA Modules:
  0.0 60.2 jit_solution(1810163925018918124)
XLA Ops:
  0.6 55.3 %shard_map.121 = (bf16[64,640]{1,0:T(8,128)(2,1)}, bf16[64,640]{1,0:T(8,128)(2,1)}, f32[2,16]{1,0:T(2,128)}) custom-call(s32[1,256]{1,0:T(1,128)} %bitcast.6, s32[1,256]{1,0:T(1,128)} %bitcast.7, s32[6,64]{1,0:T(8,128)} %bitcast.5, s32[1,64]{1,0:T(1,128)} %bitcast.8, f32[2,16]{1,0:T(2,128)} %adm_ref.1, f32[1,64]{1,0:T(1,128)} %bitcast.9, ...), custom_call_target="tpu_custom_call" | custom-call | tf_op jit(solution)/shard_map/pallas_call | solution.py:422
  56.0 1.5 %copy.16 = bf16[64,640]{1,0:T(8,128)(2,1)} copy(bf16[64,640]{1,0:T(8,128)(2,1)} %get-tuple-element.6) | data formatting | bytes 163840
  57.5 1.5 %copy.17 = bf16[64,640]{1,0:T(8,128)(2,1)} copy(bf16[64,640]{1,0:T(8,128)(2,1)} %get-tuple-element.7) | data formatting | bytes 163840
  59.0 1.2 %copy.18 = f32[2,16]{1,0:T(2,128)} copy(f32[2,16]{1,0:T(2,128)} %get-tuple-element.8) | data formatting | bytes 256
where the time goes:
time: 60.5 us; the launch traced here: 60.2 us
  Pallas kernels  55.3 us (91%)
  local copies, waits for them, and re-layouts  4.26 us (7%)
  between operations  0.64 us (1%)
    pallas_call x1, Pallas kernels, local(): pl.pallas_call(functools.partial(kernel, n), out_shape=(jax.ShapeDtypeStr...  55.3 us
    unnamed x3, local copies, waits for them, and re-layouts  4.26 us

commit v1 on v0

--- a/solution.py
+++ b/solution.py
@@ -398,6 +398,15 @@
             halo_copy(s, 1, down).wait_send()
 
 
+def finish(state_in, adjoint_in, grad_in, state_out, adjoint_out, grad_out, sems):
+    pairs = ((state_in, state_out), (adjoint_in, adjoint_out), (grad_in, grad_out))
+    moves = [pltpu.make_async_copy(a, b, sems.at[i]) for i, (a, b) in enumerate(pairs)]
+    for move in moves:
+        move.start()
+    for move in moves:
+        move.wait()
+
+
 def solution(mesh):
     n = mesh.shape["mesh"]
 
@@ -418,13 +427,13 @@
         lin = admittance.shape[1]
         vmem = pl.BlockSpec(memory_space=pltpu.VMEM)
         dma = pltpu.SemaphoreType.DMA
-        return tuple(
+        parts = tuple(
             pl.pallas_call(
                 functools.partial(kernel, n),
                 out_shape=(
-                    jax.ShapeDtypeStruct((elems, width), BF16),
-                    jax.ShapeDtypeStruct((elems, width), BF16),
-                    jax.ShapeDtypeStruct((2, lin), F32),
+                    pltpu.VMEM((elems, width), BF16),
+                    pltpu.VMEM((elems, width), BF16),
+                    pltpu.VMEM((2, lin), F32),
                 ),
                 in_specs=[vmem] * 7 + [pl.BlockSpec(memory_space=pltpu.HBM)] * 3,
                 out_specs=(vmem,) * 3,
@@ -457,9 +466,9 @@
                     dma((3,)),
                 ],
                 compiler_params=pltpu.CompilerParams(
-                    collective_id=0, has_side_effects=True, vmem_limit_bytes=2**26 - 2**16
+                    collective_id=0, has_side_effects=True, vmem_limit_bytes=2**26 - 2**21
                 ),
-            )(
+            )(*(pltpu.with_memory_space_constraint(x, pltpu.HBM) for x in (
                 src_owner.reshape(1, rows),
                 src_slot.reshape(1, rows),
                 neighbour_offset.T,
@@ -470,7 +479,18 @@
                 coupling,
                 block_inv,
                 liner_op,
-            )
+            )))
+        )
+        hbm = pl.BlockSpec(memory_space=pl.ANY)
+        return tuple(
+            pl.pallas_call(
+                finish,
+                out_shape=tuple(jax.ShapeDtypeStruct(x.shape, x.dtype) for x in parts),
+                in_specs=[hbm] * 3,
+                out_specs=(hbm,) * 3,
+                scratch_shapes=[pltpu.SemaphoreType.DMA((3,))],
+                compiler_params=pltpu.CompilerParams(vmem_limit_bytes=2**20),
+            )(*parts)
         )
 
     placed = (

time: 60.5 us -> 56.3 us (0.931)
  local copies, waits for them, and re-layouts: 4.26 us -> 0 us
    unnamed x3 -> x0, local copies, waits for them, and re-layouts: 4.26 us -> none
    pallas_call x1 -> x2, Pallas kernels: 55.3 us -> 55.4 us  [the longest x1 54.7 us: local(): pl.pallas_call(functools.partial(kernel, n), out_shape=(pltpu.VMEM((elems...]
where the time goes in v1:
time: 56.3 us; the launch traced here: 56.2 us
  Pallas kernels  55.4 us (98%)
  between operations  0.8 us (1%)
    pallas_call x1, Pallas kernels, local(): pl.pallas_call(functools.partial(kernel, n), out_shape=(pltpu.VMEM((elems...  54.7 us

profile of v1, /device:TPU:0, one launch (start us, length us, event | category | flops | bytes accessed | tf_op | source)
XLA Modules:
  0.0 56.2 jit_solution(12743322041880128869)
XLA Ops:
  0.6 54.7 %shard_map.121 = (bf16[64,640]{1,0:T(8,128)(2,1)S(1)}, bf16[64,640]{1,0:T(8,128)(2,1)S(1)}, f32[2,16]{1,0:T(2,128)S(1)}) custom-call(s32[1,256]{1,0:T(1,128)} %bitcast.6, s32[1,256]{1,0:T(1,128)} %bitcast.7, s32[6,64]{1,0:T(8,128)} %bitcast.5, s32[1,64]{1,0:T(1,128)} %bitcast.8, f32[2,16]{1,0:T(2,128)} %adm_ref.1, f32[1,64]{1,0:T(1,128)} %bitcast.9, ...), custom_call_target="tpu_custom_call" | custom-call | tf_op jit(solution)/shard_map/pallas_call | solution.py:431
  55.3 0.7 %shard_map.122 = (bf16[64,640]{1,0:T(8,128)(2,1)}, bf16[64,640]{1,0:T(8,128)(2,1)}, f32[2,16]{1,0:T(2,128)}) custom-call(bf16[64,640]{1,0:T(8,128)(2,1)S(1)} %get-tuple-element.6.state_in, bf16[64,640]{1,0:T(8,128)(2,1)S(1)} %get-tuple-element.7.adjoint_in, f32[2,16]{1,0:T(2,128)S(1)} %get-tuple-element.8.grad_in), custom_call_target="tpu_custom_call" | custom-call | tf_op jit(solution)/shard_map/pallas_call | solution.py:486

commit v2 on v1

v2 whole, which is shorter than its diff:
```python
import functools

import jax
import jax.numpy as jnp
from jax import lax
from jax.experimental import pallas as pl
from jax.experimental.pallas import tpu as pltpu
from jax.sharding import PartitionSpec as P

SWEEPS = 4
RIM = 16
FACES = 6
QUAD = 4
LANES = 128
MESH = pl.DeviceIdType.MESH
F32 = jnp.float32
BF16 = jnp.bfloat16


def iota(shape, dim):
    return lax.broadcasted_iota(jnp.int32, shape, dim)


def dot(a, b):
    return jnp.dot(a, b, preferred_element_type=F32)


def swap(x):
    return pltpu.roll(x, x.shape[1] // 2, 1)


def first(x):
    return iota(x.shape, 1) < x.shape[1] // 2


def times_i(x):
    turned = swap(x)
    return jnp.where(first(x), -turned, turned)


def full(x):
    x = x.astype(F32)
    return jnp.concatenate([x, times_i(x)], axis=0)


def kernel(
    n,
    owner_hbm,
    slot_hbm,
    off_hbm,
    face_hbm,
    adm_hbm,
    weight_hbm,
    src_hbm,
    coupling_hbm,
    inv_hbm,
    liner_hbm,
    state_ref,
    adjoint_ref,
    grad_ref,
    owner_ref,
    slot_ref,
    off_ref,
    face_ref,
    adm_ref,
    weight_ref,
    src_ref,
    coupling_ref,
    inv_ref,
    liner_ref,
    load_sems,
    far_send,
    near_send,
    mid,
    summed,
    near_recv,
    far_recv,
    mid_sems,
    near_sems,
    far_sems,
    adm_send,
    adm_recv,
    adm_sems,
    off_send,
    off_halo,
    off_sems,
    grad_send,
    grad_recv,
    grad_sems,
    ext,
    halo_sems,
    start_ref,
    field_re,
    field_im,
    wall_re,
    wall_im,
    inv_full,
    inv_herm,
    liner_full,
    w_fwd,
    w_adj,
    pick_fwd_ends,
    pick_adj_ends,
    pick_fwd_mid,
    pick_adj_mid,
):
    me = lax.axis_index("mesh")
    elems = off_ref.shape[1]
    nb, width = inv_ref.shape
    lin = adm_ref.shape[1]
    rows = src_ref.shape[0]
    faces = adm_send.shape[1]
    wide = wall_re.shape[1]
    quads = n // QUAD
    pieces = summed.shape[1]
    piece = elems // pieces
    own = pl.ds(elems, elems)

    up, down = jnp.minimum(me + 1, n - 1), jnp.maximum(me - 1, 0)
    has_up, has_down = me < n - 1, me > 0

    barrier = pltpu.get_barrier_semaphore()
    for k in range(1, n):
        pl.semaphore_signal(
            barrier, inc=1, device_id={"mesh": lax.rem(me + k, n)}, device_id_type=MESH
        )

    loads = [
        pltpu.make_async_copy(hbm, here, load_sems.at[i])
        for i, (hbm, here) in enumerate(
            (
                (owner_hbm, owner_ref),
                (slot_hbm, slot_ref),
                (src_hbm, src_ref),
                (off_hbm, off_ref),
                (face_hbm, face_ref),
                (weight_hbm, weight_ref),
                (adm_hbm, adm_ref),
                (inv_hbm, inv_ref),
                (coupling_hbm, coupling_ref),
                (liner_hbm, liner_ref),
            )
        )
    ]
    for load in loads:
        load.start()

    def to(src, dst, sems, at, p):
        return pltpu.make_async_remote_copy(
            src_ref=src,
            dst_ref=dst,
            send_sem=sems.at[(0, *at)],
            recv_sem=sems.at[(1, *at)],
            device_id={"mesh": p},
            device_id_type=MESH,
        )

    q, r = me // QUAD, lax.rem(me, QUAD)
    high, low = r // 2, lax.rem(r, 2)
    near = [2 * high + 1 - low, 2 * (1 - high) + low, 2 * (1 - high) + 1 - low]

    def quad_at(t):
        return lax.rem(q + t, quads)

    def mid_copy(j, t, h):
        part = pl.ds(h * piece, piece)
        return to(
            far_send.at[j, t - 1, part],
            mid.at[j, t - 1, part],
            mid_sems,
            (j, t - 1, h),
            q * QUAD + near[j],
        )

    def near_copy(j):
        return to(near_send.at[j], near_recv.at[j], near_sems, (j,), q * QUAD + near[j])

    def far_copy(t, h):
        return to(
            summed.at[t - 1, h],
            far_recv.at[t - 1, pl.ds(h * piece, piece)],
            far_sems,
            (t - 1, h),
            quad_at(t) * QUAD + r,
        )

    def adm_copy(k):
        return to(adm_send, adm_recv.at[k - 1], adm_sems, (k - 1,), lax.rem(me + k, n))

    def grad_copy(k):
        return to(grad_send, grad_recv.at[k - 1], grad_sems, (k - 1,), lax.rem(me + k, n))

    def off_copy(side):
        return to(off_send, off_halo.at[side], off_sems, (side,), up if side == 0 else down)

    def halo_copy(solve, side):
        there = pl.ds(0 if side == 0 else 2 * elems, elems)
        return to(
            ext.at[solve, own],
            ext.at[solve, there],
            halo_sems,
            (solve, side),
            up if side == 0 else down,
        )

    def each_side(copy, what, incoming):
        @pl.when(has_down if incoming else has_up)
        def _():
            getattr(copy(0), what)()

        @pl.when(has_up if incoming else has_down)
        def _():
            getattr(copy(1), what)()

    @pl.when(jnp.logical_not(has_down))
    def _():
        off_halo[0] = jnp.zeros((8, LANES), F32)
        for solve in range(2):
            ext[solve, 0:elems] = jnp.zeros((elems, width), BF16)

    @pl.when(jnp.logical_not(has_up))
    def _():
        off_halo[1] = jnp.zeros((8, LANES), F32)
        for solve in range(2):
            ext[solve, 2 * elems : 3 * elems] = jnp.zeros((elems, width), BF16)

    for load in loads[:3]:
        load.wait()
    target = owner_ref[...] * elems + slot_ref[...]

    def partial_sum(p):
        pick = (iota((elems, rows), 0) + p * elems) == target
        return dot(pick.astype(F32).astype(BF16), src_ref[...])

    for t in range(1, quads):
        for j in range(QUAD - 1):
            far_send[j, t - 1] = partial_sum(quad_at(t) * QUAD + near[j]).astype(BF16)

    for load in loads[3:7]:
        load.wait()
    off_send[...] = jnp.zeros_like(off_send)
    off_send[0:FACES, 0:elems] = off_ref[...].astype(F32)
    off_send[FACES : FACES + 1, 0:elems] = face_ref[...].astype(F32)
    off_send[FACES + 1 : FACES + 2, 0:elems] = weight_ref[...]
    adm_send[...] = jnp.zeros_like(adm_send)
    adm_send[0:2, 0:lin] = adm_ref[...]
    place = me * lin
    turned = pltpu.roll(adm_send[:, :LANES], lax.rem(place, LANES), 1)
    lane_f = iota((8, faces), 1)
    mine_f = jnp.logical_and(lane_f >= place, lane_f < place + lin)
    adm_send[...] = jnp.where(
        mine_f, jnp.concatenate([turned] * (faces // LANES), axis=1), 0.0
    )

    pl.semaphore_wait(barrier, n - 1)
    for h in range(pieces):
        for t in range(1, quads):
            for j in (2, 0, 1):
                mid_copy(j, t, h).start()
    each_side(off_copy, "start", False)
    for k in range(1, n):
        adm_copy(k).start()
    for j in (2, 0, 1):
        near_send[j] = partial_sum(q * QUAD + near[j]).astype(BF16)
        near_copy(j).start()

    loads[7].wait()
    inv_wide = full(inv_ref[...])
    inv_full[...] = inv_wide.astype(BF16)
    loads[8].wait()

    @pl.loop(0, FACES)
    def _(f):
        at = pl.ds(pl.multiple_of(f * nb, nb), nb)
        w_fwd[at, :] = dot(coupling_ref[f], inv_full[...]).astype(BF16)

    loads[9].wait()
    w_fwd[FACES * nb : (FACES + 1) * nb, :] = dot(liner_ref[...], inv_full[...]).astype(BF16)
    depth = w_fwd.shape[0]
    over = depth - (FACES + 1) * nb
    w_fwd[depth - over :, :] = jnp.zeros((over, width), BF16)
    w_adj[depth - over :, :] = jnp.zeros((over, width), BF16)

    for h in range(pieces):
        for t in range(1, quads):
            total = partial_sum(quad_at(t) * QUAD + r)[h * piece : (h + 1) * piece]
            for j in (2, 0, 1):
                mid_copy(j, t, h).wait_recv()
                total = total + mid[j, t - 1, h * piece : (h + 1) * piece].astype(F32)
            summed[t - 1, h] = total.astype(BF16)
            far_copy(t, h).start()

    def fold_adjoint(f, matrix):
        turned = dot(inv_ref[...], full(matrix).astype(BF16))
        turned = jnp.concatenate([turned, jnp.zeros((wide - nb, width), F32)], axis=0).T
        rest = jnp.zeros((nb, width - wide), F32)
        re = jnp.concatenate([turned[:nb], rest], axis=1)
        im = jnp.concatenate([turned[nb:], rest], axis=1)
        at = pl.ds(f * nb if isinstance(f, int) else pl.multiple_of(f * nb, nb), nb)
        w_adj[at, :] = (re - swap(im)).astype(BF16)

    inv_herm[...] = inv_wide.T.astype(BF16)
    liner_full[...] = full(liner_ref[...]).astype(BF16)
    fold_adjoint(FACES, liner_ref[...])

    each_side(off_copy, "wait_recv", True)
    lane = iota((8, LANES), 1)
    offs = jnp.concatenate(
        [
            jnp.where(lane < elems, off_halo[0], pltpu.roll(off_send[...], elems, 1)),
            jnp.where(lane < elems, off_halo[1], 0.0),
        ],
        axis=1,
    )
    offs_col = jnp.concatenate([offs, jnp.zeros((LANES - 8, 2 * LANES), F32)], axis=0).T

    def picks(out_lo, count, in_lo):
        place = iota((count, LANES), 0) + (out_lo - in_lo) - iota((count, LANES), 1)
        place = place.astype(F32)
        cols = offs_col[out_lo : out_lo + count]
        here = offs if in_lo == 0 else pltpu.roll(offs, 2 * LANES - in_lo, 1)
        here = here[:, :LANES]

        def hot(x):
            return jnp.where(x, 1.0, 0.0).astype(BF16)

        fwd = [hot(place + cols[:, f : f + 1] == 0.0) for f in range(FACES)]
        adj = [hot(place == here[f : f + 1, :]) for f in range(FACES)]
        return fwd, adj

    half = (3 * elems - 2 * RIM) // 2
    for side in range(2):
        fwd, adj = picks(RIM + side * half, half, side * elems)
        for f in range(FACES):
            at = pl.ds((f % 2) * LANES, LANES)
            pick_fwd_ends[side, f // 2, :, at] = fwd[f]
            pick_adj_ends[side, f // 2, :, at] = adj[f]
    mid_rows = pick_fwd_mid.shape[1]
    mid_lo = elems - (mid_rows - elems) // 2
    fwd, adj = picks(mid_lo, mid_rows, elems // 2)
    for f in range(FACES):
        at = pl.ds((f % 2) * LANES, LANES)
        pick_fwd_mid[f // 2, :, at] = fwd[f]
        pick_adj_mid[f // 2, :, at] = adj[f]

    table = adm_send[...]
    for k in range(1, n):
        adm_copy(k).wait_recv()
        table = table + adm_recv[k - 1]
    face_all = offs_col[: 3 * elems, FACES : FACES + 1]
    weight = offs_col[elems : 2 * elems, FACES + 1 : FACES + 2]
    has_face = face_all == iota((3 * elems, faces), 1).astype(F32)
    y_re = jnp.sum(jnp.where(has_face, table[0:1], 0.0), axis=1, keepdims=True)
    y_im = jnp.sum(jnp.where(has_face, table[1:2], 0.0), axis=1, keepdims=True)
    own_face = offs_col[elems : 2 * elems, FACES : FACES + 1]
    own_face = own_face == iota((elems, faces), 1).astype(F32)

    def put(lo, value, yi):
        count = value.shape[0]
        value = value.astype(BF16).astype(F32)
        turned = swap(value)
        is_re = first(value)
        at = pl.ds(lo, count)
        field_re[0, at] = jnp.where(is_re, value, 0.0).astype(BF16)
        field_re[1, at] = jnp.where(is_re, 0.0, turned).astype(BF16)
        field_im[0, at] = jnp.where(is_re, turned, 0.0).astype(BF16)
        field_im[1, at] = jnp.where(is_re, 0.0, value).astype(BF16)
        a, b = y_re[lo : lo + count], yi[lo : lo + count]
        re, im = value[:, :wide], turned[:, :wide]
        wall_re[at] = (a * re - b * im).astype(BF16)
        wall_im[at] = (a * im + b * re).astype(BF16)

    def sweep(s, ends, middle, w_ref):
        lo = RIM * s
        hi = 3 * elems - lo
        if hi - lo > mid_rows:
            centre = 3 * elems // 2
            blocks = [(ends.at[0, :, lo - RIM : half], 0), (ends.at[1, :, 0 : hi - centre], elems)]
        else:
            blocks = [(middle.at[:, lo - mid_lo : hi - mid_lo], elems // 2)]

        def met(field):
            parts = [[] for _ in range(FACES // 2)]
            for pick, in_lo in blocks:
                count = pick.shape[1]
                got = dot(
                    pick[...].reshape(FACES // 2 * count, 2 * LANES),
                    field[:, in_lo : in_lo + LANES].reshape(2 * LANES, width),
                ).astype(BF16)
                for i, part in enumerate(parts):
                    part.append(got[i * count : (i + 1) * count])
            return [jnp.concatenate(part, axis=0) for part in parts]

        left = jnp.concatenate(
            [
                jnp.concatenate(met(field_re) + [wall_re[lo:hi]], axis=1),
                jnp.concatenate(met(field_im) + [wall_im[lo:hi]], axis=1),
            ],
            axis=0,
        )
        prod = dot(left, w_ref[...])
        count = hi - lo
        return start_ref[lo:hi] - (prod[:count] + times_i(prod[count:]))

    def solve(which, start, ends, middle, w_ref, yi, beside):
        ext[which, own] = start.astype(BF16)
        each_side(lambda side: halo_copy(which, side), "start", False)
        start_ref[own] = start
        put(elems, start, yi)
        beside()
        each_side(lambda side: halo_copy(which, side), "wait_recv", True)
        for lo in (0, 2 * elems):
            halo = ext[which, lo : lo + elems].astype(F32)
            start_ref[lo : lo + elems] = halo
            put(lo, halo, yi)
        for s in range(1, SWEEPS + 1):
            now = sweep(s, ends, middle, w_ref)
            if s < SWEEPS:
                put(RIM * s, now, yi)
        return now.astype(BF16)

    forcing = partial_sum(me)
    for j in (0, 1, 2):
        near_copy(j).wait_recv()
        forcing = forcing + near_recv[j].astype(F32)
    for t in range(1, quads):
        for h in range(pieces):
            far_copy(t, h).wait_recv()
        forcing = forcing + far_recv[t - 1].astype(F32)

    def fold_rest():
        @pl.loop(0, FACES)
        def _(f):
            fold_adjoint(f, coupling_ref[f])

    state = solve(
        0,
        dot(forcing.astype(BF16), inv_full[...]),
        pick_fwd_ends,
        pick_fwd_mid,
        w_fwd,
        y_im,
        fold_rest,
    )
    source = weight * state.astype(F32)
    walls = []

    def beside():
        state_ref[...] = state
        walls.append(dot(state, liner_full[...]))

    adjoint = solve(
        1,
        dot(source.astype(BF16), inv_herm[...]),
        pick_adj_ends,
        pick_adj_mid,
        w_adj,
        -y_im,
        beside,
    )
    adjoint_f = adjoint.astype(F32)
    wall = walls[0]
    term_re = jnp.sum(adjoint_f * wall, axis=1, keepdims=True) / -16.0
    term_im = jnp.sum(adjoint_f * times_i(wall), axis=1, keepdims=True) / -16.0
    grad_re = jnp.sum(jnp.where(own_face, term_re, 0.0), axis=0, keepdims=True)
    grad_im = jnp.sum(jnp.where(own_face, term_im, 0.0), axis=0, keepdims=True)
    total = jnp.concatenate([grad_re, grad_im, jnp.zeros((6, faces), F32)], axis=0)
    grad_send[...] = total
    for k in range(1, n):
        grad_copy(k).start()
    adjoint_ref[...] = adjoint
    for k in range(1, n):
        grad_copy(k).wait_recv()
        total = total + grad_recv[k - 1]
    total = jnp.where(mine_f, total, 0.0)
    parts = [total[:, i : i + LANES] for i in range(0, faces, LANES)]
    turned = pltpu.roll(sum(parts[1:], parts[0]), LANES - lax.rem(place, LANES), 1)
    grad_ref[...] = turned[0:2, 0:lin]

    for t in range(1, quads):
        for h in range(pieces):
            for j in range(QUAD - 1):
                mid_copy(j, t, h).wait_send()
            far_copy(t, h).wait_send()
    for j in range(QUAD - 1):
        near_copy(j).wait_send()
    for k in range(1, n):
        adm_copy(k).wait_send()
        grad_copy(k).wait_send()
    each_side(off_copy, "wait_send", False)
    for which in range(2):
        each_side(lambda side: halo_copy(which, side), "wait_send", False)


def finish(state_in, adjoint_in, grad_in, state_out, adjoint_out, grad_out, sems):
    pairs = ((state_in, state_out), (adjoint_in, adjoint_out), (grad_in, grad_out))
    moves = [pltpu.make_async_copy(a, b, sems.at[i]) for i, (a, b) in enumerate(pairs)]
    for move in moves:
        move.start()
    for move in moves:
        move.wait()


def solution(mesh):
    n = mesh.shape["mesh"]

    def local(
        src_rows,
        src_owner,
        src_slot,
        neighbour_offset,
        liner_face,
        admittance,
        observe_weight,
        coupling,
        block_inv,
        liner_op,
    ):
        rows, width = src_rows.shape
        nb = width // 2
        elems = liner_face.shape[0]
        lin = admittance.shape[1]
        faces = n * lin
        quads = n // QUAD
        pieces = 2
        wide = -(-nb // LANES) * LANES
        half = (3 * elems - 2 * RIM) // 2
        others = max(quads - 1, 1)
        vmem, dma = pltpu.VMEM, pltpu.SemaphoreType.DMA
        args = (
            src_owner.reshape(1, rows),
            src_slot.reshape(1, rows),
            neighbour_offset.T,
            liner_face.reshape(1, elems),
            admittance,
            observe_weight.reshape(1, elems),
            src_rows,
            coupling,
            block_inv,
            liner_op,
        )
        parts = pl.pallas_call(
            functools.partial(kernel, n),
            out_shape=(
                vmem((elems, width), BF16),
                vmem((elems, width), BF16),
                vmem((2, lin), F32),
            ),
            in_specs=[pl.BlockSpec(memory_space=pltpu.HBM)] * len(args),
            out_specs=(pl.BlockSpec(memory_space=pltpu.VMEM),) * 3,
            scratch_shapes=[vmem(x.shape, x.dtype) for x in args]
            + [
                dma((len(args),)),
                vmem((QUAD - 1, others, elems, width), BF16),
                vmem((QUAD - 1, elems, width), BF16),
                vmem((QUAD - 1, others, elems, width), BF16),
                vmem((others, pieces, elems // pieces, width), BF16),
                vmem((QUAD - 1, elems, width), BF16),
                vmem((others, elems, width), BF16),
                dma((2, QUAD - 1, others, pieces)),
                dma((2, QUAD - 1)),
                dma((2, others, pieces)),
                vmem((8, faces), F32),
                vmem((n - 1, 8, faces), F32),
                dma((2, n - 1)),
                vmem((8, LANES), F32),
                vmem((2, 8, LANES), F32),
                dma((2, 2)),
                vmem((8, faces), F32),
                vmem((n - 1, 8, faces), F32),
                dma((2, n - 1)),
                vmem((2, 3 * elems, width), BF16),
                dma((2, 2, 2)),
                vmem((3 * elems, width), F32),
                vmem((2, 3 * elems, width), BF16),
                vmem((2, 3 * elems, width), BF16),
                vmem((3 * elems, wide), BF16),
                vmem((3 * elems, wide), BF16),
                vmem((width, width), BF16),
                vmem((width, width), BF16),
                vmem((width, width), BF16),
                vmem((FACES * nb + wide, width), BF16),
                vmem((FACES * nb + wide, width), BF16),
                vmem((2, FACES // 2, half, 2 * LANES), BF16),
                vmem((2, FACES // 2, half, 2 * LANES), BF16),
                vmem((FACES // 2, LANES - 2 * RIM, 2 * LANES), BF16),
                vmem((FACES // 2, LANES - 2 * RIM, 2 * LANES), BF16),
            ],
            compiler_params=pltpu.CompilerParams(
                collective_id=0, has_side_effects=True, vmem_limit_bytes=2**26 - 2**21
            ),
        )(*(pltpu.with_memory_space_constraint(x, pltpu.HBM) for x in args))
        anywhere = pl.BlockSpec(memory_space=pl.ANY)
        return tuple(
            pl.pallas_call(
                finish,
                out_shape=tuple(jax.ShapeDtypeStruct(x.shape, x.dtype) for x in parts),
                in_specs=[anywhere] * 3,
                out_specs=(anywhere,) * 3,
                scratch_shapes=[dma((3,))],
                compiler_params=pltpu.CompilerParams(vmem_limit_bytes=2**20),
            )(*parts)
        )

    placed = (
        P(("mode", "mesh"), None),
        P(("mode", "mesh"), None),
        P(("mode", "mesh")),
        P(("mode", "mesh"), None),
        P(("mode", "mesh")),
        P("mode", "mesh"),
        P(("mode", "mesh")),
        P("mode", None, None),
        P("mode", None),
        P("mode", None),
    )
    return jax.shard_map(
        local,
        mesh=mesh,
        in_specs=placed,
        out_specs=(P(("mode", "mesh"), None), P(("mode", "mesh"), None), P("mode", "mesh")),
        check_vma=False,
    )
```

time: 56.3 us -> 45.5 us (0.81)
  Pallas kernels: 55.4 us -> 44.5 us
    pallas_call x1, Pallas kernels: 54.7 us -> 43.8 us  [local(): pl.pallas_call(functools.partial(kernel, n), out_shape=(vmem((elems, widt...]
where the time goes in v2:
time: 45.5 us; the launch traced here: 45.3 us
  Pallas kernels  44.5 us (98%)
  between operations  0.8 us (2%)
    pallas_call x1, Pallas kernels, local(): pl.pallas_call(functools.partial(kernel, n), out_shape=(vmem((elems, widt...  43.8 us

profile of v2, /device:TPU:0, one launch (start us, length us, event | category | flops | bytes accessed | tf_op | source)
XLA Modules:
  0.0 45.3 jit_solution(1006338511953818666)
XLA Ops:
  0.6 43.8 %shard_map.121 = (bf16[64,640]{1,0:T(8,128)(2,1)S(1)}, bf16[64,640]{1,0:T(8,128)(2,1)S(1)}, f32[2,16]{1,0:T(2,128)S(1)}) custom-call(s32[1,256]{1,0:T(1,128)} %bitcast.6, s32[1,256]{1,0:T(1,128)} %bitcast.7, s32[6,64]{1,0:T(8,128)} %bitcast.5, s32[1,64]{1,0:T(1,128)} %bitcast.8, f32[2,16]{1,0:T(2,128)} %adm_hbm.1, f32[1,64]{1,0:T(1,128)} %bitcast.9, ...), custom_call_target="tpu_custom_call" | custom-call | tf_op jit(solution)/shard_map/pallas_call | solution.py:542
  44.5 0.7 %shard_map.122 = (bf16[64,640]{1,0:T(8,128)(2,1)}, bf16[64,640]{1,0:T(8,128)(2,1)}, f32[2,16]{1,0:T(2,128)}) custom-call(bf16[64,640]{1,0:T(8,128)(2,1)S(1)} %get-tuple-element.6.state_in, bf16[64,640]{1,0:T(8,128)(2,1)S(1)} %get-tuple-element.7.adjoint_in, f32[2,16]{1,0:T(2,128)S(1)} %get-tuple-element.8.grad_in), custom_call_target="tpu_custom_call" | custom-call | tf_op jit(solution)/shard_map/pallas_call | solution.py:595

commit v3 on v2

--- a/solution.py
+++ b/solution.py
@@ -110,7 +110,7 @@
     lin = adm_ref.shape[1]
     rows = src_ref.shape[0]
     faces = adm_send.shape[1]
-    wide = wall_re.shape[1]
+    wide = wall_re.shape[2]
     quads = n // QUAD
     pieces = summed.shape[1]
     piece = elems // pieces
@@ -193,13 +193,14 @@
     def off_copy(side):
         return to(off_send, off_halo.at[side], off_sems, (side,), up if side == 0 else down)
 
-    def halo_copy(solve, side):
-        there = pl.ds(0 if side == 0 else 2 * elems, elems)
+    def halo_copy(solve, reach, side):
+        mine = elems + (elems // 2 if (side == 0) == (reach == 0) else 0)
+        there = mine - elems if side == 0 else mine + elems
         return to(
-            ext.at[solve, own],
-            ext.at[solve, there],
+            ext.at[solve, pl.ds(mine, elems // 2)],
+            ext.at[solve, pl.ds(there, elems // 2)],
             halo_sems,
-            (solve, side),
+            (solve, reach, side),
             up if side == 0 else down,
         )
 
@@ -224,6 +225,8 @@
         for solve in range(2):
             ext[solve, 2 * elems : 3 * elems] = jnp.zeros((elems, width), BF16)
 
+    field_re[...] = jnp.zeros_like(field_re)
+    field_im[...] = jnp.zeros_like(field_im)
     for load in loads[:3]:
         load.wait()
     target = owner_ref[...] * elems + slot_ref[...]
@@ -299,9 +302,15 @@
         at = pl.ds(f * nb if isinstance(f, int) else pl.multiple_of(f * nb, nb), nb)
         w_adj[at, :] = (re - swap(im)).astype(BF16)
 
+    def fold_faces(begin, end):
+        @pl.loop(begin, end)
+        def _(f):
+            fold_adjoint(f, coupling_ref[f])
+
     inv_herm[...] = inv_wide.T.astype(BF16)
     liner_full[...] = full(liner_ref[...]).astype(BF16)
     fold_adjoint(FACES, liner_ref[...])
+    fold_faces(0, FACES // 3)
 
     each_side(off_copy, "wait_recv", True)
     lane = iota((8, LANES), 1)
@@ -355,68 +364,100 @@
     own_face = offs_col[elems : 2 * elems, FACES : FACES + 1]
     own_face = own_face == iota((elems, faces), 1).astype(F32)
 
-    def put(lo, value, yi):
+    def put(s, lo, value, yi):
         count = value.shape[0]
         value = value.astype(BF16).astype(F32)
         turned = swap(value)
         is_re = first(value)
-        at = pl.ds(lo, count)
-        field_re[0, at] = jnp.where(is_re, value, 0.0).astype(BF16)
-        field_re[1, at] = jnp.where(is_re, 0.0, turned).astype(BF16)
-        field_im[0, at] = jnp.where(is_re, turned, 0.0).astype(BF16)
-        field_im[1, at] = jnp.where(is_re, 0.0, value).astype(BF16)
-        a, b = y_re[lo : lo + count], yi[lo : lo + count]
+        at, b = pl.ds(lo, count), s % 2
+        field_re[b, 0, at] = jnp.where(is_re, value, 0.0).astype(BF16)
+        field_re[b, 1, at] = jnp.where(is_re, 0.0, turned).astype(BF16)
+        field_im[b, 0, at] = jnp.where(is_re, turned, 0.0).astype(BF16)
+        field_im[b, 1, at] = jnp.where(is_re, 0.0, value).astype(BF16)
+        y_r, y_i = y_re[lo : lo + count], yi[lo : lo + count]
         re, im = value[:, :wide], turned[:, :wide]
-        wall_re[at] = (a * re - b * im).astype(BF16)
-        wall_im[at] = (a * im + b * re).astype(BF16)
-
-    def sweep(s, ends, middle, w_ref):
-        lo = RIM * s
-        hi = 3 * elems - lo
-        if hi - lo > mid_rows:
-            centre = 3 * elems // 2
-            blocks = [(ends.at[0, :, lo - RIM : half], 0), (ends.at[1, :, 0 : hi - centre], elems)]
-        else:
-            blocks = [(middle.at[:, lo - mid_lo : hi - mid_lo], elems // 2)]
+        wall_re[b, at] = (y_r * re - y_i * im).astype(BF16)
+        wall_im[b, at] = (y_r * im + y_i * re).astype(BF16)
+
+    def rows_of(ref, spans):
+        parts = [ref[lo:hi] for lo, hi in spans]
+        return parts[0] if len(parts) == 1 else jnp.concatenate(parts, axis=0)
+
+    def sweep(s, blocks, w_ref):
+        b = (s - 1) % 2
+        spans = [span for block in blocks for span in block[3]]
 
         def met(field):
             parts = [[] for _ in range(FACES // 2)]
-            for pick, in_lo in blocks:
-                count = pick.shape[1]
+            for pick, base, in_lo, wanted in blocks:
+                picked = [pick[i, lo - base : hi - base] for i in range(FACES // 2) for lo, hi in wanted]
                 got = dot(
-                    pick[...].reshape(FACES // 2 * count, 2 * LANES),
-                    field[:, in_lo : in_lo + LANES].reshape(2 * LANES, width),
+                    jnp.concatenate(picked, axis=0),
+                    field[b, :, in_lo : in_lo + LANES].reshape(2 * LANES, width),
                 ).astype(BF16)
+                count = got.shape[0] // (FACES // 2)
                 for i, part in enumerate(parts):
                     part.append(got[i * count : (i + 1) * count])
-            return [jnp.concatenate(part, axis=0) for part in parts]
+            return [part[0] if len(part) == 1 else jnp.concatenate(part, axis=0) for part in parts]
 
         left = jnp.concatenate(
             [
-                jnp.concatenate(met(field_re) + [wall_re[lo:hi]], axis=1),
-                jnp.concatenate(met(field_im) + [wall_im[lo:hi]], axis=1),
+                jnp.concatenate(met(field_re) + [rows_of(wall_re.at[b], spans)], axis=1),
+                jnp.concatenate(met(field_im) + [rows_of(wall_im.at[b], spans)], axis=1),
             ],
             axis=0,
         )
         prod = dot(left, w_ref[...])
-        count = hi - lo
-        return start_ref[lo:hi] - (prod[:count] + times_i(prod[count:]))
+        count = prod.shape[0] // 2
+        return rows_of(start_ref, spans) - (prod[:count] + times_i(prod[count:]))
 
     def solve(which, start, ends, middle, w_ref, yi, beside):
         ext[which, own] = start.astype(BF16)
-        each_side(lambda side: halo_copy(which, side), "start", False)
+        for reach in range(2):
+            each_side(lambda side: halo_copy(which, reach, side), "start", False)
         start_ref[own] = start
-        put(elems, start, yi)
+        put(0, elems, start, yi)
+
+        def lower(*spans):
+            return (ends.at[0], RIM, 0, spans)
+
+        def upper(*spans):
+            return (ends.at[1], RIM + half, elems, spans)
+
+        def centre(*spans):
+            return (middle, mid_lo, elems // 2, spans)
+
+        def first_sweep(*blocks):
+            now = sweep(1, blocks, w_ref)
+            at = 0
+            for lo, hi in [span for block in blocks for span in block[3]]:
+                put(1, lo, now[at : at + hi - lo], yi)
+                at += hi - lo
+
+        def arrive(reach):
+            each_side(lambda side: halo_copy(which, reach, side), "wait_recv", True)
+            for lo in (elems // 2 * (1 - reach), 2 * elems + elems // 2 * reach):
+                halo = ext[which, lo : lo + elems // 2].astype(F32)
+                start_ref[lo : lo + elems // 2] = halo
+                put(0, lo, halo, yi)
+
+        total = 3 * elems
+        inner, near_lo, far_lo = elems + RIM, elems // 2 + RIM, RIM
         beside()
-        each_side(lambda side: halo_copy(which, side), "wait_recv", True)
-        for lo in (0, 2 * elems):
-            halo = ext[which, lo : lo + elems].astype(F32)
-            start_ref[lo : lo + elems] = halo
-            put(lo, halo, yi)
-        for s in range(1, SWEEPS + 1):
-            now = sweep(s, ends, middle, w_ref)
+        first_sweep(centre((inner, total - inner)))
+        arrive(0)
+        first_sweep(centre((near_lo, inner), (total - inner, total - near_lo)))
+        arrive(1)
+        first_sweep(lower((far_lo, near_lo)), upper((total - near_lo, total - far_lo)))
+        for s in range(2, SWEEPS + 1):
+            lo, hi = RIM * s, total - RIM * s
+            if hi - lo > mid_rows:
+                blocks = (lower((lo, total // 2)), upper((total // 2, hi)))
+            else:
+                blocks = (centre((lo, hi)),)
+            now = sweep(s, blocks, w_ref)
             if s < SWEEPS:
-                put(RIM * s, now, yi)
+                put(s, lo, now, yi)
         return now.astype(BF16)
 
     forcing = partial_sum(me)
@@ -428,11 +469,6 @@
             far_copy(t, h).wait_recv()
         forcing = forcing + far_recv[t - 1].astype(F32)
 
-    def fold_rest():
-        @pl.loop(0, FACES)
-        def _(f):
-            fold_adjoint(f, coupling_ref[f])
-
     state = solve(
         0,
         dot(forcing.astype(BF16), inv_full[...]),
@@ -440,7 +476,7 @@
         pick_fwd_mid,
         w_fwd,
         y_im,
-        fold_rest,
+        lambda: fold_faces(FACES // 3, 2 * FACES // 3),
     )
     source = weight * state.astype(F32)
     walls = []
@@ -448,6 +484,7 @@
     def beside():
         state_ref[...] = state
         walls.append(dot(state, liner_full[...]))
+        fold_faces(2 * FACES // 3, FACES)
 
     adjoint = solve(
         1,
@@ -489,7 +526,8 @@
         grad_copy(k).wait_send()
     each_side(off_copy, "wait_send", False)
     for which in range(2):
-        each_side(lambda side: halo_copy(which, side), "wait_send", False)
+        for reach in range(2):
+            each_side(lambda side: halo_copy(which, reach, side), "wait_send", False)
 
 
 def finish(state_in, adjoint_in, grad_in, state_out, adjoint_out, grad_out, sems):
@@ -570,12 +608,12 @@
                 vmem((n - 1, 8, faces), F32),
                 dma((2, n - 1)),
                 vmem((2, 3 * elems, width), BF16),
-                dma((2, 2, 2)),
+                dma((2, 2, 2, 2)),
                 vmem((3 * elems, width), F32),
-                vmem((2, 3 * elems, width), BF16),
-                vmem((2, 3 * elems, width), BF16),
-                vmem((3 * elems, wide), BF16),
-                vmem((3 * elems, wide), BF16),
+                vmem((2, 2, 3 * elems, width), BF16),
+                vmem((2, 2, 3 * elems, width), BF16),
+                vmem((2, 3 * elems, wide), BF16),
+                vmem((2, 3 * elems, wide), BF16),
                 vmem((width, width), BF16),
                 vmem((width, width), BF16),
                 vmem((width, width), BF16),

time: 45.5 us -> 42.8 us (0.941)
  Pallas kernels: 44.5 us -> 41.8 us
    pallas_call x1, Pallas kernels: 43.8 us -> 41.1 us  [local(): pl.pallas_call(functools.partial(kernel, n), out_shape=(vmem((elems, widt...]
where the time goes in v3:
time: 42.8 us; the launch traced here: 42.6 us
  Pallas kernels  41.8 us (98%)
  between operations  0.8 us (2%)
    pallas_call x1, Pallas kernels, local(): pl.pallas_call(functools.partial(kernel, n), out_shape=(vmem((elems, widt...  41.1 us

profile of v3, /device:TPU:0, one launch (start us, length us, event | category | flops | bytes accessed | tf_op | source)
XLA Modules:
  0.0 42.6 jit_solution(12190733629249338757)
XLA Ops:
  0.6 41.1 %shard_map.121 = (bf16[64,640]{1,0:T(8,128)(2,1)S(1)}, bf16[64,640]{1,0:T(8,128)(2,1)S(1)}, f32[2,16]{1,0:T(2,128)S(1)}) custom-call(s32[1,256]{1,0:T(1,128)} %bitcast.6, s32[1,256]{1,0:T(1,128)} %bitcast.7, s32[6,64]{1,0:T(8,128)} %bitcast.5, s32[1,64]{1,0:T(1,128)} %bitcast.8, f32[2,16]{1,0:T(2,128)} %adm_hbm.1, f32[1,64]{1,0:T(1,128)} %bitcast.9, ...), custom_call_target="tpu_custom_call" | custom-call | tf_op jit(solution)/shard_map/pallas_call | solution.py:580
  41.8 0.7 %shard_map.122 = (bf16[64,640]{1,0:T(8,128)(2,1)}, bf16[64,640]{1,0:T(8,128)(2,1)}, f32[2,16]{1,0:T(2,128)}) custom-call(bf16[64,640]{1,0:T(8,128)(2,1)S(1)} %get-tuple-element.6.state_in, bf16[64,640]{1,0:T(8,128)(2,1)S(1)} %get-tuple-element.7.adjoint_in, f32[2,16]{1,0:T(2,128)S(1)} %get-tuple-element.8.grad_in), custom_call_target="tpu_custom_call" | custom-call | tf_op jit(solution)/shard_map/pallas_call | solution.py:633

commit v4 on v3

--- a/solution.py
+++ b/solution.py
@@ -103,6 +103,7 @@
     pick_adj_ends,
     pick_fwd_mid,
     pick_adj_mid,
+    admit_ref,
 ):
     me = lax.axis_index("mesh")
     elems = off_ref.shape[1]
@@ -239,6 +240,30 @@
         for j in range(QUAD - 1):
             far_send[j, t - 1] = partial_sum(quad_at(t) * QUAD + near[j]).astype(BF16)
 
+    depth = w_fwd.shape[0]
+    over = depth - (FACES + 1) * nb
+
+    def fold_forward():
+        for load in loads[7:]:
+            load.wait()
+        inv_full[...] = full(inv_ref[...]).astype(BF16)
+
+        @pl.loop(0, FACES)
+        def _(f):
+            at = pl.ds(pl.multiple_of(f * nb, nb), nb)
+            w_fwd[at, :] = dot(coupling_ref[f], inv_full[...]).astype(BF16)
+
+        w_fwd[FACES * nb : depth - over, :] = dot(liner_ref[...], inv_full[...]).astype(BF16)
+        w_fwd[depth - over :, :] = jnp.zeros((over, width), BF16)
+        w_adj[depth - over :, :] = jnp.zeros((over, width), BF16)
+
+    sends_first = lax.rem(lax.axis_index("mode"), 2) == 0
+
+    pl.semaphore_wait(barrier, n - 1)
+    for h in range(pieces):
+        for t in range(1, quads):
+            for j in (2, 0, 1):
+                mid_copy(j, t, h).start()
     for load in loads[3:7]:
         load.wait()
     off_send[...] = jnp.zeros_like(off_send)
@@ -255,43 +280,25 @@
         mine_f, jnp.concatenate([turned] * (faces // LANES), axis=1), 0.0
     )
 
-    pl.semaphore_wait(barrier, n - 1)
-    for h in range(pieces):
-        for t in range(1, quads):
-            for j in (2, 0, 1):
-                mid_copy(j, t, h).start()
     each_side(off_copy, "start", False)
     for k in range(1, n):
         adm_copy(k).start()
     for j in (2, 0, 1):
         near_send[j] = partial_sum(q * QUAD + near[j]).astype(BF16)
-        near_copy(j).start()
-
-    loads[7].wait()
-    inv_wide = full(inv_ref[...])
-    inv_full[...] = inv_wide.astype(BF16)
-    loads[8].wait()
-
-    @pl.loop(0, FACES)
-    def _(f):
-        at = pl.ds(pl.multiple_of(f * nb, nb), nb)
-        w_fwd[at, :] = dot(coupling_ref[f], inv_full[...]).astype(BF16)
-
-    loads[9].wait()
-    w_fwd[FACES * nb : (FACES + 1) * nb, :] = dot(liner_ref[...], inv_full[...]).astype(BF16)
-    depth = w_fwd.shape[0]
-    over = depth - (FACES + 1) * nb
-    w_fwd[depth - over :, :] = jnp.zeros((over, width), BF16)
-    w_adj[depth - over :, :] = jnp.zeros((over, width), BF16)
-
+    near_copy(0).start()
+    fold_forward()
+
+    far_own = [partial_sum(quad_at(t) * QUAD + r) for t in range(1, quads)]
     for h in range(pieces):
         for t in range(1, quads):
-            total = partial_sum(quad_at(t) * QUAD + r)[h * piece : (h + 1) * piece]
+            total = far_own[t - 1][h * piece : (h + 1) * piece]
             for j in (2, 0, 1):
                 mid_copy(j, t, h).wait_recv()
                 total = total + mid[j, t - 1, h * piece : (h + 1) * piece].astype(F32)
             summed[t - 1, h] = total.astype(BF16)
             far_copy(t, h).start()
+    near_copy(2).start()
+    near_copy(1).start()
 
     def fold_adjoint(f, matrix):
         turned = dot(inv_ref[...], full(matrix).astype(BF16))
@@ -307,7 +314,7 @@
         def _(f):
             fold_adjoint(f, coupling_ref[f])
 
-    inv_herm[...] = inv_wide.T.astype(BF16)
+    inv_herm[...] = full(inv_ref[...]).T.astype(BF16)
     liner_full[...] = full(liner_ref[...]).astype(BF16)
     fold_adjoint(FACES, liner_ref[...])
     fold_faces(0, FACES // 3)
@@ -364,20 +371,36 @@
     own_face = offs_col[elems : 2 * elems, FACES : FACES + 1]
     own_face = own_face == iota((elems, faces), 1).astype(F32)
 
-    def put(s, lo, value, yi):
+    admit_ref[0] = jnp.broadcast_to(y_re, (3 * elems, LANES))
+    admit_ref[1] = jnp.broadcast_to(y_im, (3 * elems, LANES))
+    admit_ref[2] = jnp.broadcast_to(-y_im, (3 * elems, LANES))
+    split = nb // LANES * LANES
+
+    def put(which, s, lo, value):
         count = value.shape[0]
-        value = value.astype(BF16).astype(F32)
         turned = swap(value)
-        is_re = first(value)
         at, b = pl.ds(lo, count), s % 2
-        field_re[b, 0, at] = jnp.where(is_re, value, 0.0).astype(BF16)
-        field_re[b, 1, at] = jnp.where(is_re, 0.0, turned).astype(BF16)
-        field_im[b, 0, at] = jnp.where(is_re, turned, 0.0).astype(BF16)
-        field_im[b, 1, at] = jnp.where(is_re, 0.0, value).astype(BF16)
-        y_r, y_i = y_re[lo : lo + count], yi[lo : lo + count]
-        re, im = value[:, :wide], turned[:, :wide]
-        wall_re[b, at] = (y_r * re - y_i * im).astype(BF16)
-        wall_im[b, at] = (y_r * im + y_i * re).astype(BF16)
+        is_re = iota((count, wide - split), 1) < nb - split
+
+        def keep(ref, side, x):
+            part = x[:, split:wide]
+            if side == 0:
+                ref[b, 0, at, 0:split] = x[:, :split].astype(BF16)
+                ref[b, 0, at, split:wide] = jnp.where(is_re, part, 0.0).astype(BF16)
+            else:
+                ref[b, 1, at, split:wide] = jnp.where(is_re, 0.0, part).astype(BF16)
+                ref[b, 1, at, wide:width] = x[:, wide:].astype(BF16)
+
+        keep(field_re, 0, value)
+        keep(field_re, 1, turned)
+        keep(field_im, 0, turned)
+        keep(field_im, 1, value)
+        y_r = admit_ref[0, at]
+        y_i = admit_ref[1 + which, at]
+        for c in range(0, wide, LANES):
+            re, im = value[:, c : c + LANES], turned[:, c : c + LANES]
+            wall_re[b, at, c : c + LANES] = (y_r * re - y_i * im).astype(BF16)
+            wall_im[b, at, c : c + LANES] = (y_r * im + y_i * re).astype(BF16)
 
     def rows_of(ref, spans):
         parts = [ref[lo:hi] for lo, hi in spans]
@@ -385,53 +408,71 @@
 
     def sweep(s, blocks, w_ref):
         b = (s - 1) % 2
-        spans = [span for block in blocks for span in block[3]]
-
-        def met(field):
-            parts = [[] for _ in range(FACES // 2)]
-            for pick, base, in_lo, wanted in blocks:
-                picked = [pick[i, lo - base : hi - base] for i in range(FACES // 2) for lo, hi in wanted]
-                got = dot(
-                    jnp.concatenate(picked, axis=0),
-                    field[b, :, in_lo : in_lo + LANES].reshape(2 * LANES, width),
-                ).astype(BF16)
-                count = got.shape[0] // (FACES // 2)
-                for i, part in enumerate(parts):
-                    part.append(got[i * count : (i + 1) * count])
-            return [part[0] if len(part) == 1 else jnp.concatenate(part, axis=0) for part in parts]
-
+        spans = [span for pieces, _ in blocks for _, _, span in pieces]
+
+        parts = [[] for _ in range(FACES)]
+        for pieces, taken in blocks:
+            picked = [
+                pick[i, lo - base : hi - base]
+                for i in range(FACES // 2)
+                for pick, base, (lo, hi) in pieces
+            ]
+            given = [
+                jnp.concatenate([field[b, i, lo:hi] for i in range(2) for lo, hi in taken], axis=0)
+                for field in (field_re, field_im)
+            ]
+            got = dot(jnp.concatenate(picked, axis=0), jnp.concatenate(given, axis=1)).astype(BF16)
+            count = got.shape[0] // (FACES // 2)
+            for i, part in enumerate(parts):
+                row, lane = i % (FACES // 2) * count, i // (FACES // 2) * width
+                part.append(got[row : row + count, lane : lane + width])
+        met = [part[0] if len(part) == 1 else jnp.concatenate(part, axis=0) for part in parts]
         left = jnp.concatenate(
             [
-                jnp.concatenate(met(field_re) + [rows_of(wall_re.at[b], spans)], axis=1),
-                jnp.concatenate(met(field_im) + [rows_of(wall_im.at[b], spans)], axis=1),
+                jnp.concatenate(met[: FACES // 2] + [rows_of(wall_re.at[b], spans)], axis=1),
+                jnp.concatenate(met[FACES // 2 :] + [rows_of(wall_im.at[b], spans)], axis=1),
             ],
             axis=0,
         )
         prod = dot(left, w_ref[...])
         count = prod.shape[0] // 2
-        return rows_of(start_ref, spans) - (prod[:count] + times_i(prod[count:]))
-
-    def solve(which, start, ends, middle, w_ref, yi, beside):
+        rest = rows_of(start_ref, spans) - prod[:count]
+        turned = swap(prod[count:])
+        is_re = iota((count, wide - split), 1) < nb - split
+        part = turned[:, split:wide]
+        return jnp.concatenate(
+            [
+                rest[:, :split] + turned[:, :split],
+                rest[:, split:wide] + jnp.where(is_re, part, -part),
+                rest[:, wide:] - turned[:, wide:],
+            ],
+            axis=1,
+        )
+
+    def solve(which, start, ends, middle, w_ref, beside):
         ext[which, own] = start.astype(BF16)
         for reach in range(2):
             each_side(lambda side: halo_copy(which, reach, side), "start", False)
         start_ref[own] = start
-        put(0, elems, start, yi)
-
-        def lower(*spans):
-            return (ends.at[0], RIM, 0, spans)
-
-        def upper(*spans):
-            return (ends.at[1], RIM + half, elems, spans)
+        put(which, 0, elems, start)
+
+        total = 3 * elems
+
+        def lower(span):
+            return (ends.at[0], RIM, span)
+
+        def upper(span):
+            return (ends.at[1], RIM + half, span)
 
         def centre(*spans):
-            return (middle, mid_lo, elems // 2, spans)
+            taken = (elems // 2, elems // 2 + LANES)
+            return [(middle, mid_lo, span) for span in spans], [taken]
 
         def first_sweep(*blocks):
             now = sweep(1, blocks, w_ref)
             at = 0
-            for lo, hi in [span for block in blocks for span in block[3]]:
-                put(1, lo, now[at : at + hi - lo], yi)
+            for lo, hi in [span for pieces, _ in blocks for _, _, span in pieces]:
+                put(which, 1, lo, now[at : at + hi - lo])
                 at += hi - lo
 
         def arrive(reach):
@@ -439,25 +480,28 @@
             for lo in (elems // 2 * (1 - reach), 2 * elems + elems // 2 * reach):
                 halo = ext[which, lo : lo + elems // 2].astype(F32)
                 start_ref[lo : lo + elems // 2] = halo
-                put(0, lo, halo, yi)
-
-        total = 3 * elems
+                put(which, 0, lo, halo)
+
         inner, near_lo, far_lo = elems + RIM, elems // 2 + RIM, RIM
         beside()
         first_sweep(centre((inner, total - inner)))
         arrive(0)
         first_sweep(centre((near_lo, inner), (total - inner, total - near_lo)))
         arrive(1)
-        first_sweep(lower((far_lo, near_lo)), upper((total - near_lo, total - far_lo)))
+        outer = [lower((far_lo, near_lo)), upper((total - near_lo, total - far_lo))]
+        first_sweep((outer, [(0, elems), (total - elems, total)]))
         for s in range(2, SWEEPS + 1):
             lo, hi = RIM * s, total - RIM * s
             if hi - lo > mid_rows:
-                blocks = (lower((lo, total // 2)), upper((total // 2, hi)))
+                blocks = (
+                    ([lower((lo, total // 2))], [(0, LANES)]),
+                    ([upper((total // 2, hi))], [(total - LANES, total)]),
+                )
             else:
                 blocks = (centre((lo, hi)),)
             now = sweep(s, blocks, w_ref)
             if s < SWEEPS:
-                put(s, lo, now, yi)
+                put(which, s, lo, now)
         return now.astype(BF16)
 
     forcing = partial_sum(me)
@@ -475,16 +519,31 @@
         pick_fwd_ends,
         pick_fwd_mid,
         w_fwd,
-        y_im,
         lambda: fold_faces(FACES // 3, 2 * FACES // 3),
     )
     source = weight * state.astype(F32)
+
+    def sent_halo(which):
+        for reach in range(2):
+            each_side(lambda side: halo_copy(which, reach, side), "wait_send", False)
+
     walls = []
 
     def beside():
         state_ref[...] = state
         walls.append(dot(state, liner_full[...]))
         fold_faces(2 * FACES // 3, FACES)
+        for t in range(1, quads):
+            for h in range(pieces):
+                for j in range(QUAD - 1):
+                    mid_copy(j, t, h).wait_send()
+                far_copy(t, h).wait_send()
+        for j in range(QUAD - 1):
+            near_copy(j).wait_send()
+        for k in range(1, n):
+            adm_copy(k).wait_send()
+        each_side(off_copy, "wait_send", False)
+        sent_halo(0)
 
     adjoint = solve(
         1,
@@ -492,7 +551,6 @@
         pick_adj_ends,
         pick_adj_mid,
         w_adj,
-        -y_im,
         beside,
     )
     adjoint_f = adjoint.astype(F32)
@@ -514,20 +572,9 @@
     turned = pltpu.roll(sum(parts[1:], parts[0]), LANES - lax.rem(place, LANES), 1)
     grad_ref[...] = turned[0:2, 0:lin]
 
-    for t in range(1, quads):
-        for h in range(pieces):
-            for j in range(QUAD - 1):
-                mid_copy(j, t, h).wait_send()
-            far_copy(t, h).wait_send()
-    for j in range(QUAD - 1):
-        near_copy(j).wait_send()
     for k in range(1, n):
-        adm_copy(k).wait_send()
         grad_copy(k).wait_send()
-    each_side(off_copy, "wait_send", False)
-    for which in range(2):
-        for reach in range(2):
-            each_side(lambda side: halo_copy(which, reach, side), "wait_send", False)
+    sent_halo(1)
 
 
 def finish(state_in, adjoint_in, grad_in, state_out, adjoint_out, grad_out, sems):
@@ -623,6 +670,7 @@
                 vmem((2, FACES // 2, half, 2 * LANES), BF16),
                 vmem((FACES // 2, LANES - 2 * RIM, 2 * LANES), BF16),
                 vmem((FACES // 2, LANES - 2 * RIM, 2 * LANES), BF16),
+                vmem((3, 3 * elems, LANES), F32),
             ],
             compiler_params=pltpu.CompilerParams(
                 collective_id=0, has_side_effects=True, vmem_limit_bytes=2**26 - 2**21

time: 42.8 us -> 42.1 us (0.984)
  Pallas kernels: 41.8 us -> 41.1 us
    pallas_call x1, Pallas kernels: 41.1 us -> 40.4 us  [local(): pl.pallas_call(functools.partial(kernel, n), out_shape=(vmem((elems, widt...]
where the time goes in v4:
time: 42.1 us; the launch traced here: 41.9 us
  Pallas kernels  41.1 us (98%)
  between operations  0.8 us (2%)
    pallas_call x1, Pallas kernels, local(): pl.pallas_call(functools.partial(kernel, n), out_shape=(vmem((elems, widt...  40.4 us

profile of v4, /device:TPU:0, one launch (start us, length us, event | category | flops | bytes accessed | tf_op | source)
XLA Modules:
  0.0 41.9 jit_solution(12641946894446305647)
XLA Ops:
  0.6 40.4 %shard_map.121 = (bf16[64,640]{1,0:T(8,128)(2,1)S(1)}, bf16[64,640]{1,0:T(8,128)(2,1)S(1)}, f32[2,16]{1,0:T(2,128)S(1)}) custom-call(s32[1,256]{1,0:T(1,128)} %bitcast.6, s32[1,256]{1,0:T(1,128)} %bitcast.7, s32[6,64]{1,0:T(8,128)} %bitcast.5, s32[1,64]{1,0:T(1,128)} %bitcast.8, f32[2,16]{1,0:T(2,128)} %adm_hbm.1, f32[1,64]{1,0:T(1,128)} %bitcast.9, ...), custom_call_target="tpu_custom_call" | custom-call | tf_op jit(solution)/shard_map/pallas_call | solution.py:627
  41.0 0.7 %shard_map.122 = (bf16[64,640]{1,0:T(8,128)(2,1)}, bf16[64,640]{1,0:T(8,128)(2,1)}, f32[2,16]{1,0:T(2,128)}) custom-call(bf16[64,640]{1,0:T(8,128)(2,1)S(1)} %get-tuple-element.6.state_in, bf16[64,640]{1,0:T(8,128)(2,1)S(1)} %get-tuple-element.7.adjoint_in, f32[2,16]{1,0:T(2,128)S(1)} %get-tuple-element.8.grad_in), custom_call_target="tpu_custom_call" | custom-call | tf_op jit(solution)/shard_map/pallas_call | solution.py:681

commit v5 on v4

--- a/solution.py
+++ b/solution.py
@@ -232,13 +232,16 @@
         load.wait()
     target = owner_ref[...] * elems + slot_ref[...]
 
-    def partial_sum(p):
-        pick = (iota((elems, rows), 0) + p * elems) == target
-        return dot(pick.astype(F32).astype(BF16), src_ref[...])
+    def partial_sums(owners):
+        picks = [(iota((elems, rows), 0) + p * elems) == target for p in owners]
+        picks = [pick.astype(F32).astype(BF16) for pick in picks]
+        got = dot(jnp.concatenate(picks, axis=0), src_ref[...])
+        return [got[i * elems : (i + 1) * elems] for i in range(len(owners))]
 
     for t in range(1, quads):
+        got = partial_sums([quad_at(t) * QUAD + near[j] for j in range(QUAD - 1)])
         for j in range(QUAD - 1):
-            far_send[j, t - 1] = partial_sum(quad_at(t) * QUAD + near[j]).astype(BF16)
+            far_send[j, t - 1] = got[j].astype(BF16)
 
     depth = w_fwd.shape[0]
     over = depth - (FACES + 1) * nb
@@ -283,12 +286,14 @@
     each_side(off_copy, "start", False)
     for k in range(1, n):
         adm_copy(k).start()
-    for j in (2, 0, 1):
-        near_send[j] = partial_sum(q * QUAD + near[j]).astype(BF16)
+    got = partial_sums([q * QUAD + near[j] for j in range(QUAD - 1)])
+    for j in range(QUAD - 1):
+        near_send[j] = got[j].astype(BF16)
+    near_copy(2).start()
     near_copy(0).start()
     fold_forward()
 
-    far_own = [partial_sum(quad_at(t) * QUAD + r) for t in range(1, quads)]
+    forcing, *far_own = partial_sums([me] + [quad_at(t) * QUAD + r for t in range(1, quads)])
     for h in range(pieces):
         for t in range(1, quads):
             total = far_own[t - 1][h * piece : (h + 1) * piece]
@@ -297,7 +302,6 @@
                 total = total + mid[j, t - 1, h * piece : (h + 1) * piece].astype(F32)
             summed[t - 1, h] = total.astype(BF16)
             far_copy(t, h).start()
-    near_copy(2).start()
     near_copy(1).start()
 
     def fold_adjoint(f, matrix):
@@ -504,7 +508,6 @@
                 put(which, s, lo, now)
         return now.astype(BF16)
 
-    forcing = partial_sum(me)
     for j in (0, 1, 2):
         near_copy(j).wait_recv()
         forcing = forcing + near_recv[j].astype(F32)

time: 42.1 us -> 41.8 us (level)
  no operation moved by 1% of the time
where the time goes in v5:
time: 41.8 us; the launch traced here: 41.7 us
  Pallas kernels  40.9 us (98%)
  between operations  0.8 us (2%)
    pallas_call x1, Pallas kernels, local(): pl.pallas_call(functools.partial(kernel, n), out_shape=(vmem((elems, widt...  40.2 us

profile of v5, /device:TPU:0, one launch (start us, length us, event | category | flops | bytes accessed | tf_op | source)
XLA Modules:
  0.0 41.7 jit_solution(16392608662030589160)
XLA Ops:
  0.6 40.2 %shard_map.121 = (bf16[64,640]{1,0:T(8,128)(2,1)S(1)}, bf16[64,640]{1,0:T(8,128)(2,1)S(1)}, f32[2,16]{1,0:T(2,128)S(1)}) custom-call(s32[1,256]{1,0:T(1,128)} %bitcast.6, s32[1,256]{1,0:T(1,128)} %bitcast.7, s32[6,64]{1,0:T(8,128)} %bitcast.5, s32[1,64]{1,0:T(1,128)} %bitcast.8, f32[2,16]{1,0:T(2,128)} %adm_hbm.1, f32[1,64]{1,0:T(1,128)} %bitcast.9, ...), custom_call_target="tpu_custom_call" | custom-call | tf_op jit(solution)/shard_map/pallas_call | solution.py:630
  40.8 0.7 %shard_map.122 = (bf16[64,640]{1,0:T(8,128)(2,1)}, bf16[64,640]{1,0:T(8,128)(2,1)}, f32[2,16]{1,0:T(2,128)}) custom-call(bf16[64,640]{1,0:T(8,128)(2,1)S(1)} %get-tuple-element.6.state_in, bf16[64,640]{1,0:T(8,128)(2,1)S(1)} %get-tuple-element.7.adjoint_in, f32[2,16]{1,0:T(2,128)S(1)} %get-tuple-element.8.grad_in), custom_call_target="tpu_custom_call" | custom-call | tf_op jit(solution)/shard_map/pallas_call | solution.py:684

commit v6 on v5

--- a/solution.py
+++ b/solution.py
@@ -283,14 +283,14 @@
         mine_f, jnp.concatenate([turned] * (faces // LANES), axis=1), 0.0
     )
 
-    each_side(off_copy, "start", False)
-    for k in range(1, n):
-        adm_copy(k).start()
     got = partial_sums([q * QUAD + near[j] for j in range(QUAD - 1)])
     for j in range(QUAD - 1):
         near_send[j] = got[j].astype(BF16)
     near_copy(2).start()
     near_copy(0).start()
+    each_side(off_copy, "start", False)
+    for k in range(1, n):
+        adm_copy(k).start()
     fold_forward()
 
     forcing, *far_own = partial_sums([me] + [quad_at(t) * QUAD + r for t in range(1, quads)])

time: 41.8 us -> 41.6 us (level)
  no operation moved by 1% of the time
where the time goes in v6:
time: 41.6 us; the launch traced here: 41.5 us
  Pallas kernels  40.7 us (98%)
  between operations  0.8 us (2%)
    pallas_call x1, Pallas kernels, local(): pl.pallas_call(functools.partial(kernel, n), out_shape=(vmem((elems, widt...  40 us

profile of v6, /device:TPU:0, one launch (start us, length us, event | category | flops | bytes accessed | tf_op | source)
XLA Modules:
  0.0 41.5 jit_solution(15676356667017736032)
XLA Ops:
  0.6 40.0 %shard_map.121 = (bf16[64,640]{1,0:T(8,128)(2,1)S(1)}, bf16[64,640]{1,0:T(8,128)(2,1)S(1)}, f32[2,16]{1,0:T(2,128)S(1)}) custom-call(s32[1,256]{1,0:T(1,128)} %bitcast.6, s32[1,256]{1,0:T(1,128)} %bitcast.7, s32[6,64]{1,0:T(8,128)} %bitcast.5, s32[1,64]{1,0:T(1,128)} %bitcast.8, f32[2,16]{1,0:T(2,128)} %adm_hbm.1, f32[1,64]{1,0:T(1,128)} %bitcast.9, ...), custom_call_target="tpu_custom_call" | custom-call | tf_op jit(solution)/shard_map/pallas_call | solution.py:630
  40.6 0.7 %shard_map.122 = (bf16[64,640]{1,0:T(8,128)(2,1)}, bf16[64,640]{1,0:T(8,128)(2,1)}, f32[2,16]{1,0:T(2,128)}) custom-call(bf16[64,640]{1,0:T(8,128)(2,1)S(1)} %get-tuple-element.6.state_in, bf16[64,640]{1,0:T(8,128)(2,1)S(1)} %get-tuple-element.7.adjoint_in, f32[2,16]{1,0:T(2,128)S(1)} %get-tuple-element.8.grad_in), custom_call_target="tpu_custom_call" | custom-call | tf_op jit(solution)/shard_map/pallas_call | solution.py:684

commit v7 on v6

--- a/solution.py
+++ b/solution.py
@@ -267,6 +267,11 @@
         for t in range(1, quads):
             for j in (2, 0, 1):
                 mid_copy(j, t, h).start()
+    got = partial_sums([q * QUAD + near[j] for j in range(QUAD - 1)])
+    for j in range(QUAD - 1):
+        near_send[j] = got[j].astype(BF16)
+    near_copy(2).start()
+    near_copy(0).start()
     for load in loads[3:7]:
         load.wait()
     off_send[...] = jnp.zeros_like(off_send)
@@ -283,11 +288,6 @@
         mine_f, jnp.concatenate([turned] * (faces // LANES), axis=1), 0.0
     )
 
-    got = partial_sums([q * QUAD + near[j] for j in range(QUAD - 1)])
-    for j in range(QUAD - 1):
-        near_send[j] = got[j].astype(BF16)
-    near_copy(2).start()
-    near_copy(0).start()
     each_side(off_copy, "start", False)
     for k in range(1, n):
         adm_copy(k).start()

time: 41.6 us -> 41.6 us (level)
  no operation moved by 1% of the time
where the time goes in v7:
time: 41.6 us; the launch traced here: 41.5 us
  Pallas kernels  40.7 us (98%)
  between operations  0.8 us (2%)
    pallas_call x1, Pallas kernels, local(): pl.pallas_call(functools.partial(kernel, n), out_shape=(vmem((elems, widt...  40 us

profile of v7, /device:TPU:0, one launch (start us, length us, event | category | flops | bytes accessed | tf_op | source)
XLA Modules:
  0.0 41.5 jit_solution(14297479063636757443)
XLA Ops:
  0.6 40.0 %shard_map.121 = (bf16[64,640]{1,0:T(8,128)(2,1)S(1)}, bf16[64,640]{1,0:T(8,128)(2,1)S(1)}, f32[2,16]{1,0:T(2,128)S(1)}) custom-call(s32[1,256]{1,0:T(1,128)} %bitcast.6, s32[1,256]{1,0:T(1,128)} %bitcast.7, s32[6,64]{1,0:T(8,128)} %bitcast.5, s32[1,64]{1,0:T(1,128)} %bitcast.8, f32[2,16]{1,0:T(2,128)} %adm_hbm.1, f32[1,64]{1,0:T(1,128)} %bitcast.9, ...), custom_call_target="tpu_custom_call" | custom-call | tf_op jit(solution)/shard_map/pallas_call | solution.py:630
  40.6 0.7 %shard_map.122 = (bf16[64,640]{1,0:T(8,128)(2,1)}, bf16[64,640]{1,0:T(8,128)(2,1)}, f32[2,16]{1,0:T(2,128)}) custom-call(bf16[64,640]{1,0:T(8,128)(2,1)S(1)} %get-tuple-element.6.state_in, bf16[64,640]{1,0:T(8,128)(2,1)S(1)} %get-tuple-element.7.adjoint_in, f32[2,16]{1,0:T(2,128)S(1)} %get-tuple-element.8.grad_in), custom_call_target="tpu_custom_call" | custom-call | tf_op jit(solution)/shard_map/pallas_call | solution.py:684
